TPU v7x, 256 devices: a whole 4x4x8 slice. The times are simulated.
256 devices in a mesh: row: 8 (over z_lo, x), col: 32 (over z_hi, y, core).
Axes of the slice: x: 4, y: 4, z: 8 (z_hi: 4, z_lo: 2; z = z_hi * 2 + z_lo), core: 2. Of those that a mesh axis runs over, the one named last changes fastest.
Arguments:
- embeddings: bfloat16 [32768, 1536], P(('row', 'col')), may hold values from -6 to 6
- membership: int32 [32768, 1], P(('row', 'col')), may hold values from 0 to 7; in each aligned block of 128 rows (0 to 127, 128 to 255, ...) at most 24 rows name the same one
- selected: int32 [8, 8], replicated, may hold values from 0 to 32767
Outputs:
- gains: float32 [32768], P(('row', 'col'))
Inputs may be any that keep to these rules, and one draw needn't show every extreme that they name: `membership`: among the 128 images of one device (aligned blocks in order), at most 24 belong to one window; some window reaches 24 images.
All inputs are finite; a program needn't handle non-finite values.
Results may differ from a plain program's by a relative error of at most 0.0003.
Values may be sent and summed in bfloat16 or wider, within the bound.
A program may use at most 64 MiB of HBM per device.

v0:
```python
import math

import jax
import jax.numpy as jnp
from jax import lax
from jax.sharding import PartitionSpec as P

GAIN_SCALE = 1.0 / 64.0


def dot_rows(left, right):
    return lax.dot_general(
        left, right, (((1,), (1,)), ((), ())), preferred_element_type=jnp.float32
    )


def coverage(points, point_win, chosen, sim_scale, windows):
    similar = dot_rows(points, chosen) * sim_scale
    best_by_window = jnp.max(similar.reshape(points.shape[0], windows, -1), axis=2)
    in_window = point_win[:, None] == jnp.arange(windows, dtype=jnp.int32)[None, :]
    return jnp.maximum(jnp.sum(jnp.where(in_window, best_by_window, 0.0), axis=1), 0.0)


def make_fold(points, point_win, cover_vals, sim_scale, pieces):
    feat_width = points.shape[1]

    def block_gain(operands):
        cand_block, win_block = operands
        tile_sims = dot_rows(cand_block, points) * sim_scale
        same_win = win_block[:, None] == point_win[None, :]
        return jnp.sum(
            jnp.where(same_win, jnp.maximum(tile_sims - cover_vals[None, :], 0.0), 0.0), axis=1
        )

    cand_rows, cand_win = pieces
    piece_rows = cand_rows.shape[0]
    block_rows = math.gcd(piece_rows, 512)
    partial_gain = lax.map(
        block_gain,
        (cand_rows.reshape(-1, block_rows, feat_width), cand_win.reshape(-1, block_rows)),
    )
    return partial_gain.reshape(-1)


def shards(embeddings, membership, selected):
    row_count, feat_width = embeddings.shape
    sim_scale = 1.0 / math.sqrt(feat_width)
    windows = selected.shape[0]
    member_ids = membership[:, 0]
    base_index = (lax.axis_index("row") * lax.axis_size("col") + lax.axis_index("col")) * row_count
    local_ids = base_index + jnp.arange(row_count, dtype=jnp.int32)
    flat_ids = selected.reshape(-1)
    picker = (flat_ids[:, None] == local_ids[None, :]).astype(jnp.bfloat16)
    chosen = jnp.dot(picker, embeddings, preferred_element_type=jnp.float32)
    chosen = lax.psum(chosen, ("row", "col")).astype(jnp.bfloat16)
    points, point_win = (
        lax.all_gather(embeddings, "row", axis=0, tiled=True),
        lax.all_gather(member_ids, "row", axis=0, tiled=True),
    )
    cover_vals = coverage(points, point_win, chosen, sim_scale, windows)
    gain_terms = make_fold(
        points,
        point_win,
        cover_vals,
        sim_scale,
        (
            lax.all_gather(embeddings, "col", axis=0, tiled=True),
            lax.all_gather(member_ids, "col", axis=0, tiled=True),
        ),
    )
    result = lax.psum_scatter(gain_terms, "col", scatter_dimension=0, tiled=True)
    return result * GAIN_SCALE


def solution(mesh):
    in_specs = (P(("row", "col"), None), P(("row", "col"), None), P())
    out_specs = P(("row", "col"))
    return jax.shard_map(shards, mesh=mesh, in_specs=in_specs, out_specs=out_specs, check_vma=False)
```

profile of v0, /device:TPU:1, one launch (start us, length us, event | category | flops | bytes accessed | tf_op | source)
XLA Modules:
  0.0 357.9 jit_solution(7849612049500457435)
XLA Ops:
  6.5 0.0 all-gather.7.cloned.1.call-start
  6.5 0.7 all-gather.7.cloned.1.call-update
  7.3 0.0 all-gather.5.cloned.1.call-start
  7.3 0.7 all-gather.5.cloned.1.call-update
  8.0 0.8 eq.46
  8.8 1.2 fusion.6
  10.1 48.8 %all-gather = s32[4096,1]{0,1:T(1,128)S(1)} all-gather(s32[128,1]{0,1:T(1,128)} %param.6), channel_id=2, replica_groups=mesh['row'=8,'col'=32] {'col'}, dimensions={0}, use_global_device_ids=true | all-gather | bytes 16896 | tf_op jit(solution)/shard_map/all_gather | solution.py:68
  58.9 0.5 broadcast.20
  59.4 0.7 reduce.3
  60.1 1.3 dynamic-slice
  62.1 14.6 %all-gather.1 = s32[1024,1]{0,1:T(1,128)S(1)} all-gather(s32[128,1]{0,1:T(1,128)} %param.6), channel_id=3, replica_groups=mesh['row'=8,'col'=32] {'row'}, dimensions={0}, use_global_device_ids=true | all-gather | bytes 4608 | tf_op jit(solution)/shard_map/all_gather | solution.py:58
  76.7 96.6 %all-reduce.2 = bf16[64,1536]{1,0:T(8,128)(2,1)S(1)} all-reduce(f32[64,1536]{1,0:T(8,128)S(1)} %fusion.6), channel_id=1, replica_groups=mesh['row'=8,'col'=32] {'row','col'}, use_global_device_ids=true, to_apply=%region_0.0 | all-reduce | flops 98304 | bytes 589824 | tf_op jit(solution)/shard_map/psum | solution.py:55
  173.2 0.0 all-gather.7.cloned.1.call-done
  173.2 0.0 copy-start
  173.3 3.1 fusion.4
  176.4 0.0 all-gather.5.cloned.1.call-done
  176.5 0.0 copy-done
  176.5 28.1 %while.10 = (s32[]{:T(128)}, f32[8,512]{1,0:T(8,128)S(1)}, s32[8,512]{1,0:T(8,128)S(1)}, s32[1024]{0:T(1024)S(1)}, bf16[8,512,1536]{2,1,0:T(8,128)(2,1)}, /*inde...) while((s32[]{:T(128)}, f32[8,512]{1,0:T(8,128)S(1)}, s32[8,512]{1,0:T(8,128)S(1)}, ...), condition=%wide.region_5.6_spmd, body=%wide.region_3.5_spmd.sunk | while | flops 1613757952 | bytes 4739685 | solution.py:38
  176.5 3.4 select_reduce_fusion.3
  179.9 0.1 dynamic_update_slice.5
  180.0 3.4 select_reduce_fusion.3
  183.4 0.1 dynamic_update_slice.5
  183.5 3.4 select_reduce_fusion.3
  186.9 0.1 dynamic_update_slice.5
  187.0 3.4 select_reduce_fusion.3
  190.5 0.1 dynamic_update_slice.5
  190.6 3.4 select_reduce_fusion.3
  194.0 0.1 dynamic_update_slice.5
  194.1 3.4 select_reduce_fusion.3
  197.5 0.1 dynamic_update_slice.5
  197.6 3.4 select_reduce_fusion.3
  201.0 0.1 dynamic_update_slice.5
  201.1 3.4 select_reduce_fusion.3
  204.5 0.1 dynamic_update_slice.5
  204.6 145.8 %all-reduce = f32[4096]{0:T(1024)S(1)} all-reduce(f32[4096]{0:T(1024)S(1)} %bitcast.29), channel_id=4, replica_groups=mesh['row'=8,'col'=32] {'col'}, use_global_device_ids=true, to_apply=%region_6.7.clone | all-reduce | flops 4096 | bytes 32768
  350.5 0.6 dynamic-slice_multiply_fusion
  (14 shorter events, 0.1 us)
Async XLA Ops:
  6.5 166.7 %all-gather.7.cloned.1.call-start = ((), (), s32[]{:S(2)}) async-start(), calls=%async_computation.1 | async-start | bytes 3538944 | tf_op jit(solution)/shard_map/all_gather | solution.py:57
  7.3 169.2 %all-gather.5.cloned.1.call-start = ((), (), s32[]{:S(2)}) async-start(), calls=%async_computation | async-start | bytes 12976128 | tf_op jit(solution)/shard_map/all_gather | solution.py:67
  173.2 3.2 copy-start
Sparse Core Ops, SparseCore 0:
  9.1 48.1 all-gather.6
  59.9 102.5 all-gather.4
where the time goes:
time: 362 us; the launch traced here: 358 us
  blocking collectives  306 us (85%)
  matrix products  31.7 us (9%)
  between operations  14.2 us (4%)
    unnamed x1, blocking collectives  146 us
    psum x1, blocking collectives, shards(): chosen = lax.psum(chosen, ('row', 'col')).astype(jnp.bfloat16)  96.6 us
    all_gather x1, blocking collectives, shards(): lax.all_gather(member_ids, 'col', axis=0, tiled=True)  48.8 us
    dot_general x9, matrix products, dot_rows(): lax.dot_general(left, right, (((1,), (1,)), ((), ())), preferred_element_...  30.5 us
    all_gather x1, blocking collectives, shards(): lax.all_gather(member_ids, 'row', axis=0, tiled=True)  14.6 us
  transfers between devices with their start and end apart: 2, of which 0 were waited for; matrix products, arithmetic and copies ran while one was open for 2% of the time, Pallas kernels for 0%

commit v1 on v0

v1 whole, which is shorter than its diff:
```python
import functools
import math

import jax
import jax.numpy as jnp
from jax import lax
from jax.experimental import pallas as pl
from jax.experimental.pallas import tpu as pltpu
from jax.sharding import PartitionSpec as P

GAIN_SCALE = 1.0 / 64.0
MESH = pl.DeviceIdType.MESH
F32, BF16, I32 = jnp.float32, jnp.bfloat16, jnp.int32

CAP = 24
WIN = 8
PICKS = 8
RING = 4
WAVES = (0, 1, 7, 2, 6, 3, 5, 4)
ZK, XP, XM, X3, YP, YM, Y3, K0 = range(8)


def coords():
    row, col = lax.axis_index("row"), lax.axis_index("col")
    x, z_lo = lax.rem(row, 4), lax.div(row, 4)
    z_hi, y, k = lax.div(col, 8), lax.rem(lax.div(col, 2), 4), lax.rem(col, 2)
    return x, y, z_hi * 2 + z_lo, k


def device(x, y, z, k):
    return lax.rem(z, 2) * 4 + x, lax.div(z, 2) * 8 + y * 2 + k


def rows_dot(left, right):
    return lax.dot_general(left, right, (((1,), (1,)), ((), ())), preferred_element_type=F32)


def kernel(
    emb, mem, sel, out,
    sort, pick, rawx, rawy, raws, s1r, s2s, s2r, s3r, s3s, s4r, chosen,
    points, cands, cov, acc, gs, gy, ts, gz,
    wsend, wrecv, csend, crecv, gsend, grecv,
):
    x, y, z, k = coords()
    rows, width = emb.shape
    half = width // 2
    scale = 1.0 / math.sqrt(width)
    q = x * 2 + k

    def at(dx=0, dy=0, dz=0, dk=0):
        return device(
            lax.rem(x + dx, 4), lax.rem(y + dy, 4), lax.rem(z + dz, 8), lax.rem(k + dk, 2)
        )

    def at_q(d):
        other = lax.rem(q + d, 8)
        return device(lax.div(other, 2), y, z, lax.rem(other, 2))

    def copy(src, dst, ssem, rsem, to):
        return pltpu.make_async_remote_copy(
            src_ref=src, dst_ref=dst, send_sem=ssem, recv_sem=rsem, device_id=to, device_id_type=MESH
        )

    barrier = pltpu.get_barrier_semaphore()
    peers = [at(dz=d) for d in range(1, 8)] + [at_q(d) for d in range(1, 8)] + [at(dy=d) for d in range(1, 4)]
    for peer in peers:
        pl.semaphore_signal(barrier, inc=1, device_id=peer, device_id_type=MESH)

    win = mem[...]
    up = lax.rem(z - win + 8, 8)
    wave = jnp.where(up == 0, 0, jnp.where(up <= 4, 2 * up - 1, 16 - 2 * up))
    in_wave = lax.broadcasted_iota(I32, (WIN, rows), 0) == wave
    before = lax.broadcasted_iota(I32, (rows, rows), 0) < lax.broadcasted_iota(I32, (rows, rows), 1)
    ahead = jnp.dot(
        jnp.where(in_wave, 1.0, 0.0).astype(BF16), jnp.where(before, 1.0, 0.0).astype(BF16),
        preferred_element_type=F32,
    )
    place = jnp.sum(jnp.where(in_wave, ahead, 0.0), axis=0, keepdims=True).astype(I32)
    slot = wave * CAP + place
    slots = WIN * CAP
    sorter = jnp.where(lax.broadcasted_iota(I32, (slots, rows), 0) == slot, 1.0, 0.0)
    base = (lax.axis_index("row") * 32 + lax.axis_index("col")) * rows
    local = base + lax.broadcasted_iota(I32, (PICKS, rows), 1)
    eye = lax.broadcasted_iota(I32, (PICKS, PICKS), 0) == lax.broadcasted_iota(I32, (PICKS, PICKS), 1)
    pickers = []
    for g in range(WIN):
        ids = jnp.sum(jnp.where(eye, sel[g : g + 1, :].astype(F32), 0.0), axis=1, keepdims=True)
        pickers.append(jnp.where(local == ids.astype(I32), 1.0, 0.0))
    onehot = jnp.concatenate([sorter] + pickers, axis=0).astype(BF16)
    low = jnp.dot(onehot, emb[:, :half], preferred_element_type=F32)
    high = jnp.dot(onehot, emb[:, half:], preferred_element_type=F32)
    for g in range(WIN):
        lo, hi = slots + g * PICKS, slots + (g + 1) * PICKS
        pick[g] = jnp.concatenate([low[lo:hi], high[lo:hi]], axis=0).astype(BF16)
    for n in range(WIN):
        lo, hi = n * CAP, (n + 1) * CAP
        part = jnp.concatenate([low[lo:hi], high[lo:hi]], axis=0).astype(BF16)
        if n == 0:
            rawx[0, 0] = part
        else:
            sort[n - 1] = part
    acc[...] = jnp.zeros_like(acc)

    pl.semaphore_wait(barrier, len(peers))

    started = []

    def start(cp):
        cp.start()
        started.append(cp)
        return cp

    picks1 = []
    for d in range(1, 8):
        g = lax.rem(z - lax.rem(q + d, 8) + 8, 8)
        picks1.append(start(copy(pick.at[g], s1r.at[d - 1], csend.at[d - 1], crecv.at[d - 1], at_q(d))))

    def zcopy(n):
        return start(
            copy(sort.at[n - 1], rawx.at[n, 0], wsend.at[n, ZK], wrecv.at[n, ZK], at(dz=8 - WAVES[n]))
        )

    wave_copies = {}

    def wcopy(n, kind, src, dst, to):
        wave_copies[n, kind] = start(copy(src, dst, wsend.at[n, kind], wrecv.at[n, kind], to))

    def level0(n):
        if n > 0:
            zs[n].wait_recv()
        own = rawx.at[n, 0]
        wcopy(n, XP, own, rawx.at[n, 1], at(dx=1))
        wcopy(n, YP, own, rawy.at[n, 0], at(dy=1))
        wcopy(n, XM, own, rawx.at[n, 2], at(dx=3))
        wcopy(n, YM, own, rawy.at[n, 1], at(dy=3))
        wcopy(n, K0, own, raws.at[n, 0], at(dk=1))

    def level1(n):
        first, second = ((XP, YP, 1), (XM, YM, 2)) if n % 2 == 0 else ((XM, YM, 2), (XP, YP, 1))
        xk, yk, s = first
        on = 1 if s == 1 else 3
        wave_copies[n, xk].wait_recv()
        wcopy(n, X3, rawx.at[n, s], rawx.at[n, 3], at(dx=on))
        wcopy(n, K0 + s, rawx.at[n, s], raws.at[n, s], at(dk=1))
        wave_copies[n, yk].wait_recv()
        wcopy(n, Y3, rawy.at[n, s - 1], rawy.at[n, 2], at(dy=on))
        xk, yk, s = second
        wave_copies[n, xk].wait_recv()
        wcopy(n, K0 + s, rawx.at[n, s], raws.at[n, s], at(dk=1))
        wave_copies[n, yk].wait_recv()

    def level2(n):
        wave_copies[n, X3].wait_recv()
        wcopy(n, K0 + 3, rawx.at[n, 3], raws.at[n, 3], at(dk=1))
        wave_copies[n, Y3].wait_recv()

    def level3(n):
        for s in range(RING):
            wave_copies[n, K0 + s].wait_recv()

    def chosen1():
        total = pick[lax.rem(z - q + 8, 8)].astype(F32)
        for d in range(7):
            picks1[d].wait_recv()
            total = total + s1r[d].astype(F32)
        s2s[...] = total.astype(BF16)
        cp = copy(s2s, s2r, csend.at[7], crecv.at[7], at(dz=8 - q))

        @pl.when(q == 0)
        def _():
            s2r[...] = s2s[...]

        @pl.when(q != 0)
        def _():
            cp.start()

        return cp

    def chosen2(cp):
        @pl.when(q != 0)
        def _():
            cp.wait()

        return [
            start(copy(s2r, s3r.at[d - 1], csend.at[7 + d], crecv.at[7 + d], at(dy=d))) for d in range(1, 4)
        ]

    def chosen3(cps):
        total = s2r[...].astype(F32)
        for d in range(3):
            cps[d].wait_recv()
            total = total + s3r[d].astype(F32)
        s3s[...] = total.astype(BF16)
        return [
            start(copy(s3s, s4r.at[d - 1], csend.at[10 + d], crecv.at[10 + d], at_q(d))) for d in range(1, 8)
        ]

    def chosen4(cps):
        total = s3s[...].astype(F32)
        for d in range(7):
            cps[d].wait_recv()
            total = total + s4r[d].astype(F32)
        whole = jnp.concatenate([total[:PICKS], total[PICKS:]], axis=1)
        chosen[...] = jnp.concatenate([whole, whole], axis=0).astype(BF16)

    pair = 2 * CAP
    prow, crow = 2 * RING * pair, RING * pair

    def assemble(group):
        def put(dst, row, ref, s):
            a, b = ref[2 * group, s].astype(F32), ref[2 * group + 1, s].astype(F32)
            dst[row : row + pair, :half] = jnp.concatenate([a[:CAP], b[:CAP]], axis=0).astype(BF16)
            dst[row : row + pair, half:] = jnp.concatenate([a[CAP:], b[CAP:]], axis=0).astype(BF16)

        for s in range(RING):
            put(points, group * prow + s * pair, rawx, s)
            put(points, group * prow + crow + s * pair, raws, s)
            put(cands, group * crow + s * pair, *((rawx, 0) if s == 0 else (rawy, s - 1)))

    def cover(group):
        near = rows_dot(points[group * prow : (group + 1) * prow, :], chosen[...]) * scale
        cov[group * prow : (group + 1) * prow, :] = jnp.maximum(jnp.max(near, axis=1, keepdims=True), 0.0)

    def unit(a, b):
        lo = pl.multiple_of(a * prow, prow)
        sims = rows_dot(points[pl.ds(lo, prow), :], cands[pl.ds(pl.multiple_of(b * crow, crow), crow), :])
        terms = jnp.maximum(sims * scale - cov[pl.ds(lo, prow), :], 0.0)
        acc[b] += jnp.sum(terms.reshape(prow // 8, 8, crow), axis=0)

    def fold(group):
        assemble(group)
        cover(group)

        def body(i, carry):
            a = jnp.where(i <= group, group, i - group - 1)
            b = jnp.where(i <= group, i, group)
            unit(a, b)
            return carry

        lax.fori_loop(0, 2 * group + 1, body, 0)

    zs = {n: zcopy(n) for n in (1, 2, 3, 4)}
    level0(0)
    c2 = chosen1()
    level0(1)
    level1(0)
    zs[5] = zcopy(5)
    level0(2)
    zs[6] = zcopy(6)
    c3 = chosen2(c2)
    level1(1)
    level2(0)
    level0(3)
    zs[7] = zcopy(7)
    level1(2)
    level2(1)
    c4 = chosen3(c3)
    level0(4)
    level1(3)
    level2(2)
    level0(5)
    level1(4)
    level2(3)
    chosen4(c4)
    level3(0)
    level3(1)
    fold(0)
    level0(6)
    level1(5)
    level2(4)
    level3(2)
    level3(3)
    fold(1)
    level0(7)
    level1(6)
    level2(5)
    level1(7)
    level2(6)
    level3(4)
    level3(5)
    fold(2)
    level2(7)
    level3(6)
    level3(7)
    fold(3)

    groups = WIN // 2
    part = jnp.concatenate(
        [jnp.sum(acc[b], axis=0, keepdims=True) for b in range(groups)] + [jnp.zeros((8 - groups, crow), F32)], axis=0
    )
    gs[...] = jnp.concatenate([part, jnp.zeros((8, 256 - crow), F32)], axis=1)
    back = [start(copy(gs, gy.at[i], gsend.at[i], grecv.at[i], at(dy=d))) for i, d in enumerate((1, 3, 2))]
    total = gs[...]
    for i, s in enumerate((2, 1, 3)):
        back[i].wait_recv()
        total = total + pltpu.roll(gy[i], 256 - s * pair, 1)
    ts[...] = total[:, :128]
    home = [
        start(copy(ts, gz.at[n - 1], gsend.at[2 + n], grecv.at[2 + n], at(dz=WAVES[n]))) for n in range(1, 8)
    ]
    row_id = lax.broadcasted_iota(I32, (8, 128), 0)
    lane = lax.broadcasted_iota(I32, (8, 128), 1)
    shift = lax.rem(wave, 2) * CAP + place
    spread = jnp.where(lax.broadcasted_iota(I32, (128, rows), 0) == shift, 1.0, 0.0)
    gathered = jnp.zeros((8, 128), F32)
    for n in range(8):
        if n > 0:
            home[n - 1].wait_recv()
        got = ts[...] if n == 0 else gz[n - 1]
        first = (n % 2) * CAP
        here = (row_id == n // 2) & (lane >= first) & (lane < first + CAP)
        gathered = gathered + jnp.where(here, got, 0.0)
    placed = jnp.dot(gathered, spread, precision=lax.Precision.HIGHEST, preferred_element_type=F32)
    mine = lax.broadcasted_iota(I32, (8, rows), 0) == lax.div(wave, 2)
    out[...] = jnp.sum(jnp.where(mine, placed, 0.0), axis=0, keepdims=True) * GAIN_SCALE
    for cp in started:
        cp.wait_send()


def shards(embeddings, membership, selected):
    rows, width = embeddings.shape
    half = width // 2
    chunk, short = (2 * CAP, half), (2 * PICKS, half)
    dma = pltpu.SemaphoreType.DMA
    vmem = pl.BlockSpec(memory_space=pltpu.VMEM)
    gains = pl.pallas_call(
        kernel,
        out_shape=jax.ShapeDtypeStruct((1, rows), F32),
        in_specs=[vmem] * 3,
        out_specs=vmem,
        scratch_shapes=[
            pltpu.VMEM((7,) + chunk, BF16),
            pltpu.VMEM((8,) + short, BF16),
            pltpu.VMEM((8, 4) + chunk, BF16),
            pltpu.VMEM((8, 3) + chunk, BF16),
            pltpu.VMEM((8, 4) + chunk, BF16),
            pltpu.VMEM((7,) + short, BF16),
            pltpu.VMEM(short, BF16),
            pltpu.VMEM(short, BF16),
            pltpu.VMEM((3,) + short, BF16),
            pltpu.VMEM(short, BF16),
            pltpu.VMEM((7,) + short, BF16),
            pltpu.VMEM((2 * PICKS, width), BF16),
            pltpu.VMEM((8 * 8 * CAP, width), BF16),
            pltpu.VMEM((8 * 4 * CAP, width), BF16),
            pltpu.VMEM((8 * 8 * CAP, 1), F32),
            pltpu.VMEM((4, 8, 8 * CAP), F32),
            pltpu.VMEM((8, 256), F32),
            pltpu.VMEM((3, 8, 256), F32),
            pltpu.VMEM((8, 128), F32),
            pltpu.VMEM((7, 8, 128), F32),
            dma((8, 11)), dma((8, 11)), dma((18,)), dma((18,)), dma((10,)), dma((10,)),
        ],
        compiler_params=pltpu.CompilerParams(
            collective_id=0, has_side_effects=True, vmem_limit_bytes=40 * 1024 * 1024
        ),
    )(embeddings, membership.reshape(1, rows), selected)
    return gains.reshape(rows)


def solution(mesh):
    in_specs = (P(("row", "col"), None), P(("row", "col"), None), P())
    out_specs = P(("row", "col"))
    return jax.shard_map(shards, mesh=mesh, in_specs=in_specs, out_specs=out_specs, check_vma=False)
```

time: 362 us -> 61.8 us (0.17); the launches traced: 358 us -> 61.6 us
  blocking collectives: 306 us -> 0 us
  Pallas kernels: 0 us -> 58.7 us
  matrix products: 31.7 us -> 0 us
  between operations: 14.2 us -> 0.01 us
    unnamed x1 -> x0, blocking collectives: 146 us -> none
    psum x1 -> x0, blocking collectives: 96.6 us -> none  [shards(): chosen = lax.psum(chosen, ('row', 'col')).astype(jnp.bfloat16)]
    all_gather x2 -> x0, blocking collectives: 63.4 us -> none  [the longest x1 48.8 us: shards(): lax.all_gather(member_ids, 'col', axis=0, tiled=True)]
    pallas_call x0 -> x1, Pallas kernels: none -> 58.7 us  [shards(): pl.pallas_call(kernel, out_shape=jax.ShapeDtypeStruct((1, rows), F32), in...]
    dot_general x10 -> x0, matrix products: 31.7 us -> none  [the longest x9 30.5 us: dot_rows(): lax.dot_general(left, right, (((1,), (1,)), ((), ())), preferred_element_...]
  transfers between devices with their start and end apart: 2 -> 0, of which waited for: 0 -> 0; matrix products, arithmetic and copies ran while one was open for 2% -> 0% of each run, Pallas kernels for 0% -> 0%
where the time goes in v1:
time: 61.8 us; the launch traced here: 61.6 us
  Pallas kernels  58.7 us (95%)
  local copies, waits for them, and re-layouts  2.85 us (5%)
    pallas_call x1, Pallas kernels, shards(): pl.pallas_call(kernel, out_shape=jax.ShapeDtypeStruct((1, rows), F32), in...  58.7 us
    unnamed x7, local copies, waits for them, and re-layouts  2.85 us

profile of v1, /device:TPU:1, one launch (start us, length us, event | category | flops | bytes accessed | tf_op | source)
XLA Modules:
  0.0 61.6 jit_solution(6124673627568686005)
XLA Ops:
  0.0 0.0 copy-start.2
  0.0 0.7 %copy-done.2 = s32[128,1]{0,1:T(1,128)S(1)} copy-done((s32[128,1]{0,1:T(1,128)S(1)}, s32[128,1]{0,1:T(1,128)}, u32[]{:S(2)}) %copy-start.2) | copy-done | bytes 536
  0.7 0.0 copy-start
  0.7 1.0 %copy-done = bf16[128,1536]{1,0:T(8,128)(2,1)S(1)} copy-done((bf16[128,1536]{1,0:T(8,128)(2,1)S(1)}, bf16[128,1536]{1,0:T(8,128)(2,1)}, u32[]{:S(2)}) %copy-start) | copy-done | bytes 393240
  1.7 0.0 copy-start.1
  1.7 0.7 %copy-done.1 = s32[8,8]{1,0:T(8,128)S(1)} copy-done((s32[8,8]{1,0:T(8,128)S(1)}, s32[8,8]{1,0:T(8,128)}, u32[]{:S(2)}) %copy-start.1) | copy-done | bytes 280
  2.3 58.7 %shard_map.37 = f32[1,128]{1,0:T(1,128)S(1)} custom-call(bf16[128,1536]{1,0:T(8,128)(2,1)S(1)} %copy-done, s32[1,128]{1,0:T(1,128)S(1)} %bitcast.2, s32[8,8]{1,0:T(8,128)S(1)} %copy-done.1), custom_call_target="tpu_custom_call" | custom-call | tf_op jit(solution)/shard_map/pallas_call | solution.py:326
  61.1 0.5 copy.5
Async XLA Ops:
  0.0 0.7 %copy-start.2 = (s32[128,1]{0,1:T(1,128)S(1)}, s32[128,1]{0,1:T(1,128)}, u32[]{:S(2)}) copy-start(s32[128,1]{0,1:T(1,128)} %param.4) | copy-start | bytes 1540
  0.7 1.0 %copy-start = (bf16[128,1536]{1,0:T(8,128)(2,1)S(1)}, bf16[128,1536]{1,0:T(8,128)(2,1)}, u32[]{:S(2)}) copy-start(bf16[128,1536]{1,0:T(8,128)(2,1)} %emb.1) | copy-start | bytes 1179652
  1.7 0.7 %copy-start.1 = (s32[8,8]{1,0:T(8,128)S(1)}, s32[8,8]{1,0:T(8,128)}, u32[]{:S(2)}) copy-start(s32[8,8]{1,0:T(8,128)} %sel.1) | copy-start | bytes 772

commit v2 on v1

--- a/solution.py
+++ b/solution.py
@@ -17,7 +17,7 @@
 PICKS = 8
 RING = 4
 WAVES = (0, 1, 7, 2, 6, 3, 5, 4)
-ZK, XP, XM, X3, YP, YM, Y3, K0 = range(8)
+ZK, XP, XM, X3, YP, YM, Y3, KK = range(8)
 
 
 def coords():
@@ -36,10 +36,10 @@
 
 
 def kernel(
-    emb, mem, sel, out,
-    sort, pick, rawx, rawy, raws, s1r, s2s, s2r, s3r, s3s, s4r, chosen,
+    emb_in, mem_in, sel_in, out,
+    emb, mem, sel, sort, pick, rawx, rawy, raws, s1r, s2s, s2r, s3r, s3s, s4r, chosen,
     points, cands, cov, acc, gs, gy, ts, gz,
-    wsend, wrecv, csend, crecv, gsend, grecv,
+    loaded, zsend, xsend, ysend, ksend, psend, wrecv, crecv, gsend, grecv,
 ):
     x, y, z, k = coords()
     rows, width = emb.shape
@@ -65,6 +65,14 @@
     peers = [at(dz=d) for d in range(1, 8)] + [at_q(d) for d in range(1, 8)] + [at(dy=d) for d in range(1, 4)]
     for peer in peers:
         pl.semaphore_signal(barrier, inc=1, device_id=peer, device_id_type=MESH)
+    loads = [
+        pltpu.make_async_copy(src, dst, loaded.at[i])
+        for i, (src, dst) in enumerate(((mem_in, mem), (sel_in, sel), (emb_in, emb)))
+    ]
+    for load in loads:
+        load.start()
+    for load in loads:
+        load.wait()
 
     win = mem[...]
     up = lax.rem(z - win + 8, 8)
@@ -103,27 +111,28 @@
 
     pl.semaphore_wait(barrier, len(peers))
 
-    started = []
-
     def start(cp):
         cp.start()
-        started.append(cp)
         return cp
+
+    def sent(ref, sem):
+        pltpu.make_async_copy(ref, ref, sem).wait()
 
     picks1 = []
     for d in range(1, 8):
         g = lax.rem(z - lax.rem(q + d, 8) + 8, 8)
-        picks1.append(start(copy(pick.at[g], s1r.at[d - 1], csend.at[d - 1], crecv.at[d - 1], at_q(d))))
+        picks1.append(start(copy(pick.at[g], s1r.at[d - 1], psend.at[0], crecv.at[d - 1], at_q(d))))
 
     def zcopy(n):
         return start(
-            copy(sort.at[n - 1], rawx.at[n, 0], wsend.at[n, ZK], wrecv.at[n, ZK], at(dz=8 - WAVES[n]))
+            copy(sort.at[n - 1], rawx.at[n, 0], zsend, wrecv.at[n, ZK], at(dz=8 - WAVES[n]))
         )
 
     wave_copies = {}
 
     def wcopy(n, kind, src, dst, to):
-        wave_copies[n, kind] = start(copy(src, dst, wsend.at[n, kind], wrecv.at[n, kind], to))
+        sem = xsend if kind in (XP, XM, X3) else ysend if kind in (YP, YM, Y3) else ksend
+        wave_copies[n, kind] = start(copy(src, dst, sem, wrecv.at[n, kind], to))
 
     def level0(n):
         if n > 0:
@@ -133,30 +142,24 @@
         wcopy(n, YP, own, rawy.at[n, 0], at(dy=1))
         wcopy(n, XM, own, rawx.at[n, 2], at(dx=3))
         wcopy(n, YM, own, rawy.at[n, 1], at(dy=3))
-        wcopy(n, K0, own, raws.at[n, 0], at(dk=1))
 
     def level1(n):
-        first, second = ((XP, YP, 1), (XM, YM, 2)) if n % 2 == 0 else ((XM, YM, 2), (XP, YP, 1))
-        xk, yk, s = first
-        on = 1 if s == 1 else 3
+        xk, yk, s, on = (XP, YP, 1, 1) if n % 2 == 0 else (XM, YM, 2, 3)
         wave_copies[n, xk].wait_recv()
         wcopy(n, X3, rawx.at[n, s], rawx.at[n, 3], at(dx=on))
-        wcopy(n, K0 + s, rawx.at[n, s], raws.at[n, s], at(dk=1))
         wave_copies[n, yk].wait_recv()
         wcopy(n, Y3, rawy.at[n, s - 1], rawy.at[n, 2], at(dy=on))
-        xk, yk, s = second
-        wave_copies[n, xk].wait_recv()
-        wcopy(n, K0 + s, rawx.at[n, s], raws.at[n, s], at(dk=1))
-        wave_copies[n, yk].wait_recv()
+        wave_copies[n, XP + XM - xk].wait_recv()
+        wcopy(n, KK, rawx.at[n, pl.ds(0, 3)], raws.at[n, pl.ds(0, 3)], at(dk=1))
+        wave_copies[n, YP + YM - yk].wait_recv()
 
     def level2(n):
         wave_copies[n, X3].wait_recv()
-        wcopy(n, K0 + 3, rawx.at[n, 3], raws.at[n, 3], at(dk=1))
+        wcopy(n, KK, rawx.at[n, 3], raws.at[n, 3], at(dk=1))
         wave_copies[n, Y3].wait_recv()
 
     def level3(n):
-        for s in range(RING):
-            wave_copies[n, K0 + s].wait_recv()
+        sent(raws.at[n], wrecv.at[n, KK])
 
     def chosen1():
         total = pick[lax.rem(z - q + 8, 8)].astype(F32)
@@ -164,7 +167,7 @@
             picks1[d].wait_recv()
             total = total + s1r[d].astype(F32)
         s2s[...] = total.astype(BF16)
-        cp = copy(s2s, s2r, csend.at[7], crecv.at[7], at(dz=8 - q))
+        cp = copy(s2s, s2r, psend.at[1], crecv.at[7], at(dz=8 - q))
 
         @pl.when(q == 0)
         def _():
@@ -182,7 +185,7 @@
             cp.wait()
 
         return [
-            start(copy(s2r, s3r.at[d - 1], csend.at[7 + d], crecv.at[7 + d], at(dy=d))) for d in range(1, 4)
+            start(copy(s2r, s3r.at[d - 1], psend.at[2], crecv.at[7 + d], at(dy=d))) for d in range(1, 4)
         ]
 
     def chosen3(cps):
@@ -192,7 +195,7 @@
             total = total + s3r[d].astype(F32)
         s3s[...] = total.astype(BF16)
         return [
-            start(copy(s3s, s4r.at[d - 1], csend.at[10 + d], crecv.at[10 + d], at_q(d))) for d in range(1, 8)
+            start(copy(s3s, s4r.at[d - 1], psend.at[3], crecv.at[10 + d], at_q(d))) for d in range(1, 8)
         ]
 
     def chosen4(cps):
@@ -228,7 +231,6 @@
         acc[b] += jnp.sum(terms.reshape(prow // 8, 8, crow), axis=0)
 
     def fold(group):
-        assemble(group)
         cover(group)
 
         def body(i, carry):
@@ -239,49 +241,60 @@
 
         lax.fori_loop(0, 2 * group + 1, body, 0)
 
-    zs = {n: zcopy(n) for n in (1, 2, 3, 4)}
+    zs = {n: zcopy(n) for n in (1, 2)}
     level0(0)
+    zs.update({n: zcopy(n) for n in (3, 4)})
+    level0(1)
+    level0(2)
+    zs.update({n: zcopy(n) for n in (5, 6)})
+    level1(0)
     c2 = chosen1()
-    level0(1)
-    level1(0)
-    zs[5] = zcopy(5)
-    level0(2)
-    zs[6] = zcopy(6)
+    level0(3)
+    level0(4)
+    zs[7] = zcopy(7)
+    level1(1)
+    level1(2)
+    level2(0)
     c3 = chosen2(c2)
-    level1(1)
-    level2(0)
-    level0(3)
-    zs[7] = zcopy(7)
-    level1(2)
+    level0(5)
+    level0(6)
+    level1(3)
+    level1(4)
     level2(1)
+    level2(2)
     c4 = chosen3(c3)
-    level0(4)
-    level1(3)
-    level2(2)
-    level0(5)
-    level1(4)
-    level2(3)
-    chosen4(c4)
     level3(0)
     level3(1)
+    assemble(0)
+    level0(7)
+    level1(5)
+    level1(6)
+    level2(3)
+    level2(4)
+    chosen4(c4)
     fold(0)
-    level0(6)
-    level1(5)
-    level2(4)
     level3(2)
     level3(3)
+    assemble(1)
+    level1(7)
+    level2(5)
+    level2(6)
     fold(1)
-    level0(7)
-    level1(6)
-    level2(5)
-    level1(7)
-    level2(6)
     level3(4)
     level3(5)
+    assemble(2)
+    level2(7)
     fold(2)
-    level2(7)
+    sent(sort, zsend)
+    sent(rawy, xsend)
+    sent(rawy, ysend)
+    sent(raws, ksend)
+    sent(s1r, psend.at[0])
+    sent(s3r, psend.at[2])
+    sent(s4r, psend.at[3])
     level3(6)
     level3(7)
+    assemble(3)
     fold(3)
 
     groups = WIN // 2
@@ -289,14 +302,14 @@
         [jnp.sum(acc[b], axis=0, keepdims=True) for b in range(groups)] + [jnp.zeros((8 - groups, crow), F32)], axis=0
     )
     gs[...] = jnp.concatenate([part, jnp.zeros((8, 256 - crow), F32)], axis=1)
-    back = [start(copy(gs, gy.at[i], gsend.at[i], grecv.at[i], at(dy=d))) for i, d in enumerate((1, 3, 2))]
+    back = [start(copy(gs, gy.at[i], gsend.at[0], grecv.at[i], at(dy=d))) for i, d in enumerate((1, 3, 2))]
     total = gs[...]
     for i, s in enumerate((2, 1, 3)):
         back[i].wait_recv()
         total = total + pltpu.roll(gy[i], 256 - s * pair, 1)
     ts[...] = total[:, :128]
     home = [
-        start(copy(ts, gz.at[n - 1], gsend.at[2 + n], grecv.at[2 + n], at(dz=WAVES[n]))) for n in range(1, 8)
+        start(copy(ts, gz.at[n - 1], gsend.at[1], grecv.at[2 + n], at(dz=WAVES[n]))) for n in range(1, 8)
     ]
     row_id = lax.broadcasted_iota(I32, (8, 128), 0)
     lane = lax.broadcasted_iota(I32, (8, 128), 1)
@@ -313,8 +326,8 @@
     placed = jnp.dot(gathered, spread, precision=lax.Precision.HIGHEST, preferred_element_type=F32)
     mine = lax.broadcasted_iota(I32, (8, rows), 0) == lax.div(wave, 2)
     out[...] = jnp.sum(jnp.where(mine, placed, 0.0), axis=0, keepdims=True) * GAIN_SCALE
-    for cp in started:
-        cp.wait_send()
+    sent(gy, gsend.at[0])
+    sent(gz, gsend.at[1])
 
 
 def shards(embeddings, membership, selected):
@@ -322,13 +335,15 @@
     half = width // 2
     chunk, short = (2 * CAP, half), (2 * PICKS, half)
     dma = pltpu.SemaphoreType.DMA
-    vmem = pl.BlockSpec(memory_space=pltpu.VMEM)
     gains = pl.pallas_call(
         kernel,
         out_shape=jax.ShapeDtypeStruct((1, rows), F32),
-        in_specs=[vmem] * 3,
-        out_specs=vmem,
+        in_specs=[pl.BlockSpec(memory_space=pltpu.HBM)] * 3,
+        out_specs=pl.BlockSpec(memory_space=pltpu.VMEM),
         scratch_shapes=[
+            pltpu.VMEM((rows, width), BF16),
+            pltpu.VMEM((1, rows), I32),
+            pltpu.VMEM(selected.shape, I32),
             pltpu.VMEM((7,) + chunk, BF16),
             pltpu.VMEM((8,) + short, BF16),
             pltpu.VMEM((8, 4) + chunk, BF16),
@@ -349,10 +364,10 @@
             pltpu.VMEM((3, 8, 256), F32),
             pltpu.VMEM((8, 128), F32),
             pltpu.VMEM((7, 8, 128), F32),
-            dma((8, 11)), dma((8, 11)), dma((18,)), dma((18,)), dma((10,)), dma((10,)),
+            dma((3,)), dma, dma, dma, dma, dma((4,)), dma((8, 8)), dma((18,)), dma((2,)), dma((10,)),
         ],
         compiler_params=pltpu.CompilerParams(
-            collective_id=0, has_side_effects=True, vmem_limit_bytes=40 * 1024 * 1024
+            collective_id=0, has_side_effects=True, vmem_limit_bytes=62 * 1024 * 1024
         ),
     )(embeddings, membership.reshape(1, rows), selected)
     return gains.reshape(rows)

time: 61.8 us -> 56 us (0.906); the launches traced: 61.6 us -> 55.2 us
  Pallas kernels: 58.7 us -> 54.1 us
  local copies, waits for them, and re-layouts: 2.85 us -> 1.1 us
    pallas_call x1, Pallas kernels: 58.7 us -> 54.1 us  [shards(): pl.pallas_call(kernel, out_shape=jax.ShapeDtypeStruct((1, rows), F32), in...]
    unnamed x7 -> x3, local copies, waits for them, and re-layouts: 2.85 us -> 1.1 us
where the time goes in v2:
time: 56 us; the launch traced here: 55.2 us
  Pallas kernels  54.1 us (97%)
  local copies, waits for them, and re-layouts  1.1 us (2%)
    pallas_call x1, Pallas kernels, shards(): pl.pallas_call(kernel, out_shape=jax.ShapeDtypeStruct((1, rows), F32), in...  54.1 us

profile of v2, /device:TPU:1, one launch (start us, length us, event | category | flops | bytes accessed | tf_op | source)
XLA Modules:
  0.0 55.2 jit_solution(12911615048615639377)
XLA Ops:
  0.0 54.1 %shard_map.37 = f32[1,128]{1,0:T(1,128)} custom-call(bf16[128,1536]{1,0:T(8,128)(2,1)} %emb_in.1, s32[1,128]{1,0:T(1,128)} %bitcast.2, s32[8,8]{1,0:T(8,128)} %sel_in.1), custom_call_target="tpu_custom_call" | custom-call | tf_op jit(solution)/shard_map/pallas_call | solution.py:338
  54.1 0.0 copy-start
  54.1 0.6 %copy-done = f32[1,128]{1,0:T(1,128)S(1)} copy-done((f32[1,128]{1,0:T(1,128)S(1)}, f32[1,128]{1,0:T(1,128)}, u32[]{:S(2)}) %copy-start) | copy-done | bytes 536
  54.7 0.5 copy.5
Async XLA Ops:
  54.1 0.6 %copy-start = (f32[1,128]{1,0:T(1,128)S(1)}, f32[1,128]{1,0:T(1,128)}, u32[]{:S(2)}) copy-start(f32[1,128]{1,0:T(1,128)} %shard_map.37) | copy-start | bytes 1540

commit v3 on v2

v3 whole, which is shorter than its diff:
```python
import functools
import math

import jax
import jax.numpy as jnp
from jax import lax
from jax.experimental import pallas as pl
from jax.experimental.pallas import tpu as pltpu
from jax.sharding import PartitionSpec as P

GAIN_SCALE = 1.0 / 64.0
MESH = pl.DeviceIdType.MESH
F32, BF16, I32 = jnp.float32, jnp.bfloat16, jnp.int32

CAP = 24
WIN = 8
PICKS = 8
RING = 4
WAVES = (0, 1, 7, 2, 6, 3, 5, 4)
BATCHES = ((0, 1), (1, 2), (3, 2), (5, 2), (7, 1))
PAIRS = ((1, 2), (3, 4), (5, 6), (7, 0))
ZK, XP, XM, X3, YP, YM, Y3, KK = range(8)


def coords():
    row, col = lax.axis_index("row"), lax.axis_index("col")
    x, z_lo = lax.rem(row, 4), lax.div(row, 4)
    z_hi, y, k = lax.div(col, 8), lax.rem(lax.div(col, 2), 4), lax.rem(col, 2)
    return x, y, z_hi * 2 + z_lo, k


def device(x, y, z, k):
    return lax.rem(z, 2) * 4 + x, lax.div(z, 2) * 8 + y * 2 + k


def rows_dot(left, right):
    return lax.dot_general(left, right, (((1,), (1,)), ((), ())), preferred_element_type=F32)


def kernel(
    emb_in, mem_in, sel_in, out,
    emb, mem, sel, sort, pick, rawx, rawy, raws, s1r, s2s, s2r, s3r, s3s, s4r, chosen,
    points, cands, cov, acc, gs, gz,
    loaded, zsend, xsend, ysend, ksend, psend, wrecv, crecv, gsend, grecv,
):
    x, y, z, k = coords()
    rows, width = emb.shape
    half = width // 2
    scale = 1.0 / math.sqrt(width)
    q = x * 2 + k

    def at(dx=0, dy=0, dz=0, dk=0):
        return device(
            lax.rem(x + dx, 4), lax.rem(y + dy, 4), lax.rem(z + dz, 8), lax.rem(k + dk, 2)
        )

    def at_q(d):
        other = lax.rem(q + d, 8)
        return device(lax.div(other, 2), y, z, lax.rem(other, 2))

    def copy(src, dst, ssem, rsem, to):
        return pltpu.make_async_remote_copy(
            src_ref=src, dst_ref=dst, send_sem=ssem, recv_sem=rsem, device_id=to, device_id_type=MESH
        )

    barrier = pltpu.get_barrier_semaphore()
    peers = [at(dz=d) for d in range(1, 8)] + [at_q(d) for d in range(1, 8)] + [at(dy=d) for d in range(1, 4)]
    loads = [
        pltpu.make_async_copy(src, dst, loaded.at[i])
        for i, (src, dst) in enumerate(((mem_in, mem), (sel_in, sel), (emb_in, emb)))
    ]
    for load in loads:
        load.start()
    for peer in peers:
        pl.semaphore_signal(barrier, inc=1, device_id=peer, device_id_type=MESH)
    for load in loads:
        load.wait()

    win = mem[...]
    up = lax.rem(z - win + 8, 8)
    wave = jnp.where(up == 0, 0, jnp.where(up <= 4, 2 * up - 1, 16 - 2 * up))
    in_wave = lax.broadcasted_iota(I32, (WIN, rows), 0) == wave
    before = lax.broadcasted_iota(I32, (rows, rows), 0) < lax.broadcasted_iota(I32, (rows, rows), 1)
    ahead = jnp.dot(
        jnp.where(in_wave, 1.0, 0.0).astype(BF16), jnp.where(before, 1.0, 0.0).astype(BF16),
        preferred_element_type=F32,
    )
    place = jnp.sum(jnp.where(in_wave, ahead, 0.0), axis=0, keepdims=True).astype(I32)
    slot = wave * CAP + place
    slots = WIN * CAP
    sorter = jnp.where(lax.broadcasted_iota(I32, (slots, rows), 0) == slot, 1.0, 0.0)
    base = (lax.axis_index("row") * 32 + lax.axis_index("col")) * rows
    local = base + lax.broadcasted_iota(I32, (PICKS, rows), 1)
    eye = lax.broadcasted_iota(I32, (PICKS, PICKS), 0) == lax.broadcasted_iota(I32, (PICKS, PICKS), 1)
    pickers = []
    for g in range(WIN):
        ids = jnp.sum(jnp.where(eye, sel[g : g + 1, :].astype(F32), 0.0), axis=1, keepdims=True)
        pickers.append(jnp.where(local == ids.astype(I32), 1.0, 0.0))
    onehot = jnp.concatenate([sorter] + pickers, axis=0).astype(BF16)
    low = jnp.dot(onehot, emb[:, :half], preferred_element_type=F32)
    high = jnp.dot(onehot, emb[:, half:], preferred_element_type=F32)
    for g in range(WIN):
        lo, hi = slots + g * PICKS, slots + (g + 1) * PICKS
        pick[g] = jnp.concatenate([low[lo:hi], high[lo:hi]], axis=0).astype(BF16)
    for n in range(WIN):
        lo, hi = n * CAP, (n + 1) * CAP
        part = jnp.concatenate([low[lo:hi], high[lo:hi]], axis=0).astype(BF16)
        if n == 0:
            rawx[0, 0] = part
        else:
            sort[n - 1] = part
    acc[...] = jnp.zeros_like(acc)

    pl.semaphore_wait(barrier, len(peers))

    def start(cp):
        cp.start()
        return cp

    def sent(ref, sem):
        pltpu.make_async_copy(ref, ref, sem).wait()

    for d in range(1, 8):
        g = lax.rem(z - lax.rem(q + d, 8) + 8, 8)
        start(copy(pick.at[g], s1r.at[d - 1], psend.at[0], crecv.at[0], at_q(d)))

    def zcopy(n):
        return start(
            copy(sort.at[n - 1], rawx.at[0, n], zsend, wrecv.at[n, ZK], at(dz=8 - WAVES[n]))
        )

    wave_copies = {}

    def wcopy(c, kind, src, dst, to):
        sem = xsend if kind in (XP, XM, X3) else ysend if kind in (YP, YM, Y3) else ksend
        wave_copies[c, kind] = start(copy(src, dst, sem, wrecv.at[c, kind], to))

    def span(c):
        return pl.ds(*BATCHES[c])

    def level0(c):
        first, count = BATCHES[c]
        for n in range(first, first + count):
            if n > 0:
                zs[n].wait_recv()
        own = rawx.at[0, span(c)]
        wcopy(c, XP, own, rawx.at[1, span(c)], at(dx=1))
        wcopy(c, YP, own, rawy.at[0, span(c)], at(dy=1))
        wcopy(c, XM, own, rawx.at[2, span(c)], at(dx=3))
        wcopy(c, YM, own, rawy.at[1, span(c)], at(dy=3))

    def level1(c):
        xk, yk, s, on = (XP, YP, 1, 1) if c % 2 == 0 else (XM, YM, 2, 3)
        wave_copies[c, xk].wait_recv()
        wcopy(c, X3, rawx.at[s, span(c)], rawx.at[3, span(c)], at(dx=on))
        wave_copies[c, yk].wait_recv()
        wcopy(c, Y3, rawy.at[s - 1, span(c)], rawy.at[2, span(c)], at(dy=on))
        wave_copies[c, XP + XM - xk].wait_recv()
        wcopy(c, KK, rawx.at[pl.ds(0, 3), span(c)], raws.at[pl.ds(0, 3), span(c)], at(dk=1))
        wave_copies[c, YP + YM - yk].wait_recv()

    def level2(c):
        wave_copies[c, X3].wait_recv()
        wcopy(c, KK, rawx.at[3, span(c)], raws.at[3, span(c)], at(dk=1))
        wave_copies[c, Y3].wait_recv()

    def level3(c):
        sent(raws.at[:, span(c)], wrecv.at[c, KK])

    def chosen1():
        sent(s1r, crecv.at[0])
        total = pick[lax.rem(z - q + 8, 8)].astype(F32) + jnp.sum(s1r[...].astype(F32), axis=0)
        s2s[...] = total.astype(BF16)

        @pl.when(q == 0)
        def _():
            s2r[...] = s2s[...]

        @pl.when(q != 0)
        def _():
            copy(s2s, s2r, psend.at[1], crecv.at[1], at(dz=8 - q)).start()

    def chosen2():
        @pl.when(q != 0)
        def _():
            copy(s2s, s2r, psend.at[1], crecv.at[1], at(dz=8 - q)).wait()

        for d in range(1, 4):
            start(copy(s2r, s3r.at[d - 1], psend.at[2], crecv.at[2], at(dy=d)))

    def chosen3():
        sent(s3r, crecv.at[2])
        total = s2r[...].astype(F32) + jnp.sum(s3r[...].astype(F32), axis=0)
        s3s[...] = total.astype(BF16)
        for d in range(1, 8):
            start(copy(s3s, s4r.at[d - 1], psend.at[3], crecv.at[3], at_q(d)))

    def chosen4():
        sent(s4r, crecv.at[3])
        total = s3s[...].astype(F32) + jnp.sum(s4r[...].astype(F32), axis=0)
        whole = jnp.concatenate([total[:PICKS], total[PICKS:]], axis=1)
        chosen[...] = jnp.concatenate([whole, whole], axis=0).astype(BF16)

    pair = 2 * CAP
    prow, crow = 2 * RING * pair, RING * pair

    def assemble(group):
        def put(dst, row, ref, s):
            a, b = ref[s, PAIRS[group][0]].astype(F32), ref[s, PAIRS[group][1]].astype(F32)
            dst[row : row + pair, :half] = jnp.concatenate([a[:CAP], b[:CAP]], axis=0).astype(BF16)
            dst[row : row + pair, half:] = jnp.concatenate([a[CAP:], b[CAP:]], axis=0).astype(BF16)

        for s in range(RING):
            put(points, group * prow + s * pair, rawx, s)
            put(points, group * prow + crow + s * pair, raws, s)
            put(cands, group * crow + s * pair, *((rawx, 0) if s == 0 else (rawy, s - 1)))

    def cover(group):
        near = rows_dot(points[group * prow : (group + 1) * prow, :], chosen[...]) * scale
        cov[group * prow : (group + 1) * prow, :] = jnp.maximum(jnp.max(near, axis=1, keepdims=True), 0.0)

    last = WIN // 2 - 1
    old_rows, old_cands = last * prow, last * crow

    def block(lo, count, left, right):
        cand = cands[left:right, :]
        terms = jnp.maximum(rows_dot(points[pl.ds(lo, count), :], cand) * scale - cov[pl.ds(lo, count), :], 0.0)
        summed = jnp.sum(terms.reshape(count // 8, 8, right - left), axis=0)
        for b in range(left // crow, right // crow):
            acc[b] += summed[:, b * crow - left : (b + 1) * crow - left]

    def fold_old():
        for group in range(last):
            cover(group)

        def body(i, carry):
            block(pl.multiple_of(i * prow, prow), prow, 0, old_cands)
            return carry

        lax.fori_loop(0, last, body, 0)

    def fold_last():
        block(0, old_rows, old_cands, old_cands + crow)
        cover(last)
        block(old_rows, prow, 0, old_cands + crow)

    zs = {n: zcopy(n) for n in (1, 2)}
    level0(0)
    zs.update({n: zcopy(n) for n in (3, 4)})
    level0(1)
    zs.update({n: zcopy(n) for n in (5, 6)})
    chosen1()
    level1(0)
    level0(2)
    zs[7] = zcopy(7)
    level1(1)
    level2(0)
    chosen2()
    level0(3)
    level1(2)
    level2(1)
    chosen3()
    level3(0)
    level3(1)
    assemble(0)
    level0(4)
    level1(3)
    level2(2)
    level3(2)
    assemble(1)
    chosen4()
    level2(3)
    level1(4)
    level3(3)
    assemble(2)
    fold_old()
    level2(4)
    sent(sort, zsend)
    sent(rawy, xsend)
    sent(rawy, ysend)
    sent(raws, ksend)
    sent(s1r, psend.at[0])
    sent(s3r, psend.at[2])
    sent(s4r, psend.at[3])
    level3(4)
    assemble(3)
    fold_last()

    for b in range(WIN // 2):
        part = jnp.sum(acc[b], axis=0, keepdims=True)
        gs[b] = jnp.concatenate([part, jnp.zeros((1, 256 - crow), F32)], axis=1)
    steps = (0, 1, 3, 2)
    for i, dy in enumerate(steps):
        for n in range(WIN):
            if i == n == 0:
                gz[0] = gs[WIN // 2 - 1]
            else:
                start(copy(gs.at[(n + 7) % 8 // 2], gz.at[i * WIN + n], gsend, grecv, at(dy=dy, dz=WAVES[n])))
    shift = lax.rem(wave + 1, 2) * CAP + place
    spread = jnp.where(lax.broadcasted_iota(I32, (128, rows), 0) == shift, 1.0, 0.0)
    mine = lax.broadcasted_iota(I32, (WIN, rows), 0) == wave
    sent(gz.at[pl.ds(1, 31)], grecv)
    total = gz[0:WIN].reshape(WIN, 256)
    for i, s in ((1, 2), (2, 1), (3, 3)):
        total = total + pltpu.roll(gz[i * WIN : (i + 1) * WIN].reshape(WIN, 256), 256 - s * pair, 1)
    placed = jnp.dot(total[:, :128], spread, precision=lax.Precision.HIGHEST, preferred_element_type=F32)
    out[...] = jnp.sum(jnp.where(mine, placed, 0.0), axis=0, keepdims=True) * GAIN_SCALE
    sent(gz.at[pl.ds(1, 31)], gsend)


def shards(embeddings, membership, selected):
    rows, width = embeddings.shape
    half = width // 2
    chunk, short = (2 * CAP, half), (2 * PICKS, half)
    dma = pltpu.SemaphoreType.DMA
    gains = pl.pallas_call(
        kernel,
        out_shape=jax.ShapeDtypeStruct((1, rows), F32),
        in_specs=[pl.BlockSpec(memory_space=pltpu.HBM)] * 3,
        out_specs=pl.BlockSpec(memory_space=pltpu.VMEM),
        scratch_shapes=[
            pltpu.VMEM((rows, width), BF16),
            pltpu.VMEM((1, rows), I32),
            pltpu.VMEM(selected.shape, I32),
            pltpu.VMEM((7,) + chunk, BF16),
            pltpu.VMEM((8,) + short, BF16),
            pltpu.VMEM((4, 8) + chunk, BF16),
            pltpu.VMEM((3, 8) + chunk, BF16),
            pltpu.VMEM((4, 8) + chunk, BF16),
            pltpu.VMEM((7,) + short, BF16),
            pltpu.VMEM(short, BF16),
            pltpu.VMEM(short, BF16),
            pltpu.VMEM((3,) + short, BF16),
            pltpu.VMEM(short, BF16),
            pltpu.VMEM((7,) + short, BF16),
            pltpu.VMEM((2 * PICKS, width), BF16),
            pltpu.VMEM((8 * 8 * CAP, width), BF16),
            pltpu.VMEM((8 * 4 * CAP, width), BF16),
            pltpu.VMEM((8 * 8 * CAP, 1), F32),
            pltpu.VMEM((4, 8, 8 * CAP), F32),
            pltpu.VMEM((4, 1, 256), F32),
            pltpu.VMEM((32, 1, 256), F32),
            dma((3,)), dma, dma, dma, dma, dma((4,)), dma((8, 8)), dma((4,)), dma, dma,
        ],
        compiler_params=pltpu.CompilerParams(
            collective_id=0, has_side_effects=True, vmem_limit_bytes=62 * 1024 * 1024
        ),
    )(embeddings, membership.reshape(1, rows), selected)
    return gains.reshape(rows)


def solution(mesh):
    in_specs = (P(("row", "col"), None), P(("row", "col"), None), P())
    out_specs = P(("row", "col"))
    return jax.shard_map(shards, mesh=mesh, in_specs=in_specs, out_specs=out_specs, check_vma=False)
```

time: 56 us -> 54.7 us (0.977); the launches traced: 55.2 us -> 54.6 us
  Pallas kernels: 54.1 us -> 53.5 us
    pallas_call x1, Pallas kernels: 54.1 us -> 53.5 us  [shards(): pl.pallas_call(kernel, out_shape=jax.ShapeDtypeStruct((1, rows), F32), in...]
where the time goes in v3:
time: 54.7 us; the launch traced here: 54.6 us
  Pallas kernels  53.5 us (98%)
  local copies, waits for them, and re-layouts  1.1 us (2%)
    pallas_call x1, Pallas kernels, shards(): pl.pallas_call(kernel, out_shape=jax.ShapeDtypeStruct((1, rows), F32), in...  53.5 us
    unnamed x3, local copies, waits for them, and re-layouts  1.1 us

profile of v3, /device:TPU:1, one launch (start us, length us, event | category | flops | bytes accessed | tf_op | source)
XLA Modules:
  0.0 54.6 jit_solution(15040524888268285962)
XLA Ops:
  0.0 53.5 %shard_map.37 = f32[1,128]{1,0:T(1,128)} custom-call(bf16[128,1536]{1,0:T(8,128)(2,1)} %emb_in.1, s32[1,128]{1,0:T(1,128)} %bitcast.2, s32[8,8]{1,0:T(8,128)} %sel_in.1), custom_call_target="tpu_custom_call" | custom-call | tf_op jit(solution)/shard_map/pallas_call | solution.py:316
  53.5 0.0 copy-start
  53.5 0.6 %copy-done = f32[1,128]{1,0:T(1,128)S(1)} copy-done((f32[1,128]{1,0:T(1,128)S(1)}, f32[1,128]{1,0:T(1,128)}, u32[]{:S(2)}) %copy-start) | copy-done | bytes 536
  54.1 0.5 copy.5
Async XLA Ops:
  53.5 0.6 %copy-start = (f32[1,128]{1,0:T(1,128)S(1)}, f32[1,128]{1,0:T(1,128)}, u32[]{:S(2)}) copy-start(f32[1,128]{1,0:T(1,128)} %shard_map.37) | copy-start | bytes 1540

commit v4 on v3

--- a/solution.py
+++ b/solution.py
@@ -39,7 +39,7 @@
 
 def kernel(
     emb_in, mem_in, sel_in, out,
-    emb, mem, sel, sort, pick, rawx, rawy, raws, s1r, s2s, s2r, s3r, s3s, s4r, chosen,
+    emb, mem, sel, sort, pick, rawx, rawy, raws, s1r, s1s, s2x, s2s, s2r, s3r, s3s, s4r, s5s, s5r, chosen,
     points, cands, cov, acc, gs, gz,
     loaded, zsend, xsend, ysend, ksend, psend, wrecv, crecv, gsend, grecv,
 ):
@@ -54,17 +54,14 @@
             lax.rem(x + dx, 4), lax.rem(y + dy, 4), lax.rem(z + dz, 8), lax.rem(k + dk, 2)
         )
 
-    def at_q(d):
-        other = lax.rem(q + d, 8)
-        return device(lax.div(other, 2), y, z, lax.rem(other, 2))
-
     def copy(src, dst, ssem, rsem, to):
         return pltpu.make_async_remote_copy(
             src_ref=src, dst_ref=dst, send_sem=ssem, recv_sem=rsem, device_id=to, device_id_type=MESH
         )
 
     barrier = pltpu.get_barrier_semaphore()
-    peers = [at(dz=d) for d in range(1, 8)] + [at_q(d) for d in range(1, 8)] + [at(dy=d) for d in range(1, 4)]
+    peers = [at(dz=d) for d in range(1, 8)] + [at(dk=1)]
+    peers += [at(dx=d) for d in range(1, 4)] + [at(dy=d) for d in range(1, 4)]
     loads = [
         pltpu.make_async_copy(src, dst, loaded.at[i])
         for i, (src, dst) in enumerate(((mem_in, mem), (sel_in, sel), (emb_in, emb)))
@@ -93,15 +90,16 @@
     local = base + lax.broadcasted_iota(I32, (PICKS, rows), 1)
     eye = lax.broadcasted_iota(I32, (PICKS, PICKS), 0) == lax.broadcasted_iota(I32, (PICKS, PICKS), 1)
     pickers = []
-    for g in range(WIN):
-        ids = jnp.sum(jnp.where(eye, sel[g : g + 1, :].astype(F32), 0.0), axis=1, keepdims=True)
+    for i in range(WIN):
+        g = lax.rem(z + 8 - ((i % 4) * 2 + i // 4), 8)
+        ids = jnp.sum(jnp.where(eye, sel[pl.ds(g, 1), :].astype(F32), 0.0), axis=1, keepdims=True)
         pickers.append(jnp.where(local == ids.astype(I32), 1.0, 0.0))
     onehot = jnp.concatenate([sorter] + pickers, axis=0).astype(BF16)
     low = jnp.dot(onehot, emb[:, :half], preferred_element_type=F32)
     high = jnp.dot(onehot, emb[:, half:], preferred_element_type=F32)
     for g in range(WIN):
         lo, hi = slots + g * PICKS, slots + (g + 1) * PICKS
-        pick[g] = jnp.concatenate([low[lo:hi], high[lo:hi]], axis=0).astype(BF16)
+        pick[g // 4, g % 4] = jnp.concatenate([low[lo:hi], high[lo:hi]], axis=0).astype(BF16)
     for n in range(WIN):
         lo, hi = n * CAP, (n + 1) * CAP
         part = jnp.concatenate([low[lo:hi], high[lo:hi]], axis=0).astype(BF16)
@@ -120,9 +118,7 @@
     def sent(ref, sem):
         pltpu.make_async_copy(ref, ref, sem).wait()
 
-    for d in range(1, 8):
-        g = lax.rem(z - lax.rem(q + d, 8) + 8, 8)
-        start(copy(pick.at[g], s1r.at[d - 1], psend.at[0], crecv.at[0], at_q(d)))
+    start(copy(pick.at[1 - k], s1r, psend.at[0], crecv.at[0], at(dk=1)))
 
     def zcopy(n):
         return start(
@@ -148,28 +144,39 @@
         wcopy(c, YP, own, rawy.at[0, span(c)], at(dy=1))
         wcopy(c, XM, own, rawx.at[2, span(c)], at(dx=3))
         wcopy(c, YM, own, rawy.at[1, span(c)], at(dy=3))
+        if c == len(BATCHES) - 1:
+            start(copy(own, rawx.at[3, span(c)], xsend, wrecv.at[c, X3], at(dx=2)))
+            start(copy(own, rawy.at[2, span(c)], ysend, wrecv.at[c, Y3], at(dy=2)))
 
     def level1(c):
-        xk, yk, s, on = (XP, YP, 1, 1) if c % 2 == 0 else (XM, YM, 2, 3)
-        wave_copies[c, xk].wait_recv()
-        wcopy(c, X3, rawx.at[s, span(c)], rawx.at[3, span(c)], at(dx=on))
-        wave_copies[c, yk].wait_recv()
-        wcopy(c, Y3, rawy.at[s - 1, span(c)], rawy.at[2, span(c)], at(dy=on))
-        wave_copies[c, XP + XM - xk].wait_recv()
+        first, count = BATCHES[c]
+        for kx, ky, s, on in ((XP, YP, 1, 1), (XM, YM, 2, 3)):
+            far = [n for n in range(first, first + count) if n % 2 == s % 2 and c < len(BATCHES) - 1]
+            wave_copies[c, kx].wait_recv()
+            for n in far:
+                start(copy(rawx.at[s, n], rawx.at[3, n], xsend, wrecv.at[c, X3], at(dx=on)))
+            wave_copies[c, ky].wait_recv()
+            for n in far:
+                start(copy(rawy.at[s - 1, n], rawy.at[2, n], ysend, wrecv.at[c, Y3], at(dy=on)))
         wcopy(c, KK, rawx.at[pl.ds(0, 3), span(c)], raws.at[pl.ds(0, 3), span(c)], at(dk=1))
-        wave_copies[c, YP + YM - yk].wait_recv()
 
     def level2(c):
-        wave_copies[c, X3].wait_recv()
+        sent(rawx.at[3, span(c)], wrecv.at[c, X3])
         wcopy(c, KK, rawx.at[3, span(c)], raws.at[3, span(c)], at(dk=1))
-        wave_copies[c, Y3].wait_recv()
+        sent(rawy.at[2, span(c)], wrecv.at[c, Y3])
 
     def level3(c):
         sent(raws.at[:, span(c)], wrecv.at[c, KK])
 
+    def chosen0():
+        sent(s1r, crecv.at[0])
+        s1s[...] = (pick[k].astype(F32) + s1r[...].astype(F32)).astype(BF16)
+        for d in range(1, 4):
+            start(copy(s1s.at[lax.rem(x + d, 4)], s2x.at[d - 1], psend.at[4], crecv.at[4], at(dx=d)))
+
     def chosen1():
-        sent(s1r, crecv.at[0])
-        total = pick[lax.rem(z - q + 8, 8)].astype(F32) + jnp.sum(s1r[...].astype(F32), axis=0)
+        sent(s2x, crecv.at[4])
+        total = s1s[x].astype(F32) + jnp.sum(s2x[...].astype(F32), axis=0)
         s2s[...] = total.astype(BF16)
 
         @pl.when(q == 0)
@@ -186,18 +193,24 @@
             copy(s2s, s2r, psend.at[1], crecv.at[1], at(dz=8 - q)).wait()
 
         for d in range(1, 4):
-            start(copy(s2r, s3r.at[d - 1], psend.at[2], crecv.at[2], at(dy=d)))
+            start(copy(s2r, s3r.at[d - 1], psend.at[2], crecv.at[2], at(dx=d)))
 
     def chosen3():
         sent(s3r, crecv.at[2])
         total = s2r[...].astype(F32) + jnp.sum(s3r[...].astype(F32), axis=0)
         s3s[...] = total.astype(BF16)
-        for d in range(1, 8):
-            start(copy(s3s, s4r.at[d - 1], psend.at[3], crecv.at[3], at_q(d)))
+        for d in range(1, 4):
+            start(copy(s3s, s4r.at[d - 1], psend.at[3], crecv.at[3], at(dy=d)))
 
     def chosen4():
         sent(s4r, crecv.at[3])
         total = s3s[...].astype(F32) + jnp.sum(s4r[...].astype(F32), axis=0)
+        s5s[...] = total.astype(BF16)
+        start(copy(s5s, s5r, psend.at[5], crecv.at[5], at(dk=1)))
+
+    def chosen5():
+        sent(s5r, crecv.at[5])
+        total = s5s[...].astype(F32) + s5r[...].astype(F32)
         whole = jnp.concatenate([total[:PICKS], total[PICKS:]], axis=1)
         chosen[...] = jnp.concatenate([whole, whole], axis=0).astype(BF16)
 
@@ -218,9 +231,6 @@
     def cover(group):
         near = rows_dot(points[group * prow : (group + 1) * prow, :], chosen[...]) * scale
         cov[group * prow : (group + 1) * prow, :] = jnp.maximum(jnp.max(near, axis=1, keepdims=True), 0.0)
-
-    last = WIN // 2 - 1
-    old_rows, old_cands = last * prow, last * crow
 
     def block(lo, count, left, right):
         cand = cands[left:right, :]
@@ -229,52 +239,70 @@
         for b in range(left // crow, right // crow):
             acc[b] += summed[:, b * crow - left : (b + 1) * crow - left]
 
-    def fold_old():
-        for group in range(last):
-            cover(group)
-
-        def body(i, carry):
-            block(pl.multiple_of(i * prow, prow), prow, 0, old_cands)
-            return carry
-
-        lax.fori_loop(0, last, body, 0)
-
-    def fold_last():
-        block(0, old_rows, old_cands, old_cands + crow)
-        cover(last)
-        block(old_rows, prow, 0, old_cands + crow)
-
-    zs = {n: zcopy(n) for n in (1, 2)}
+    def fold(p0, p1, c0, c1):
+        block(p0 * prow, (p1 - p0) * prow, c0 * crow, c1 * crow)
+
+    zs = {}
+    zs[1] = zcopy(1)
+    zs[2] = zcopy(2)
     level0(0)
-    zs.update({n: zcopy(n) for n in (3, 4)})
+    chosen0()
+    zs[3] = zcopy(3)
+    zs[4] = zcopy(4)
     level0(1)
-    zs.update({n: zcopy(n) for n in (5, 6)})
-    chosen1()
+    zs[5] = zcopy(5)
+    zs[6] = zcopy(6)
     level1(0)
     level0(2)
+    chosen1()
     zs[7] = zcopy(7)
     level1(1)
     level2(0)
+    level0(3)
     chosen2()
-    level0(3)
     level1(2)
     level2(1)
-    chosen3()
     level3(0)
     level3(1)
     assemble(0)
     level0(4)
+    chosen3()
     level1(3)
     level2(2)
+    chosen4()
     level3(2)
     assemble(1)
-    chosen4()
     level2(3)
     level1(4)
+    level2(4)
+    chosen5()
+    cover(0)
+    cover(1)
+    fold(0, 2, 0, 2)
     level3(3)
     assemble(2)
-    fold_old()
-    level2(4)
+    cover(2)
+    fold(2, 3, 0, 3)
+    fold(0, 2, 2, 3)
+    level3(4)
+    assemble(3)
+    fold(0, 3, 3, 4)
+    cover(3)
+    fold(3, 4, 0, 4)
+
+    for b in range(WIN // 2):
+        part = jnp.sum(acc[b], axis=0, keepdims=True)
+        gs[b] = jnp.concatenate([part, jnp.zeros((1, 256 - crow), F32)], axis=1)
+    steps = (0, 1, 3, 2)
+    for n in reversed(range(WIN)):
+        for i, dy in reversed(list(enumerate(steps))):
+            if i == n == 0:
+                gz[0] = gs[WIN // 2 - 1]
+            else:
+                start(copy(gs.at[(n + 7) % 8 // 2], gz.at[i * WIN + n], gsend, grecv, at(dy=dy, dz=WAVES[n])))
+    shift = lax.rem(wave + 1, 2) * CAP + place
+    spread = jnp.where(lax.broadcasted_iota(I32, (128, rows), 0) == shift, 1.0, 0.0)
+    mine = lax.broadcasted_iota(I32, (WIN, rows), 0) == wave
     sent(sort, zsend)
     sent(rawy, xsend)
     sent(rawy, ysend)
@@ -282,23 +310,8 @@
     sent(s1r, psend.at[0])
     sent(s3r, psend.at[2])
     sent(s4r, psend.at[3])
-    level3(4)
-    assemble(3)
-    fold_last()
-
-    for b in range(WIN // 2):
-        part = jnp.sum(acc[b], axis=0, keepdims=True)
-        gs[b] = jnp.concatenate([part, jnp.zeros((1, 256 - crow), F32)], axis=1)
-    steps = (0, 1, 3, 2)
-    for i, dy in enumerate(steps):
-        for n in range(WIN):
-            if i == n == 0:
-                gz[0] = gs[WIN // 2 - 1]
-            else:
-                start(copy(gs.at[(n + 7) % 8 // 2], gz.at[i * WIN + n], gsend, grecv, at(dy=dy, dz=WAVES[n])))
-    shift = lax.rem(wave + 1, 2) * CAP + place
-    spread = jnp.where(lax.broadcasted_iota(I32, (128, rows), 0) == shift, 1.0, 0.0)
-    mine = lax.broadcasted_iota(I32, (WIN, rows), 0) == wave
+    sent(s2x, psend.at[4])
+    sent(s5r, psend.at[5])
     sent(gz.at[pl.ds(1, 31)], grecv)
     total = gz[0:WIN].reshape(WIN, 256)
     for i, s in ((1, 2), (2, 1), (3, 3)):
@@ -323,16 +336,20 @@
             pltpu.VMEM((1, rows), I32),
             pltpu.VMEM(selected.shape, I32),
             pltpu.VMEM((7,) + chunk, BF16),
-            pltpu.VMEM((8,) + short, BF16),
+            pltpu.VMEM((2, 4) + short, BF16),
             pltpu.VMEM((4, 8) + chunk, BF16),
             pltpu.VMEM((3, 8) + chunk, BF16),
             pltpu.VMEM((4, 8) + chunk, BF16),
-            pltpu.VMEM((7,) + short, BF16),
-            pltpu.VMEM(short, BF16),
-            pltpu.VMEM(short, BF16),
+            pltpu.VMEM((4,) + short, BF16),
+            pltpu.VMEM((4,) + short, BF16),
             pltpu.VMEM((3,) + short, BF16),
             pltpu.VMEM(short, BF16),
-            pltpu.VMEM((7,) + short, BF16),
+            pltpu.VMEM(short, BF16),
+            pltpu.VMEM((3,) + short, BF16),
+            pltpu.VMEM(short, BF16),
+            pltpu.VMEM((3,) + short, BF16),
+            pltpu.VMEM(short, BF16),
+            pltpu.VMEM(short, BF16),
             pltpu.VMEM((2 * PICKS, width), BF16),
             pltpu.VMEM((8 * 8 * CAP, width), BF16),
             pltpu.VMEM((8 * 4 * CAP, width), BF16),
@@ -340,7 +357,7 @@
             pltpu.VMEM((4, 8, 8 * CAP), F32),
             pltpu.VMEM((4, 1, 256), F32),
             pltpu.VMEM((32, 1, 256), F32),
-            dma((3,)), dma, dma, dma, dma, dma((4,)), dma((8, 8)), dma((4,)), dma, dma,
+            dma((3,)), dma, dma, dma, dma, dma((6,)), dma((8, 8)), dma((6,)), dma, dma,
         ],
         compiler_params=pltpu.CompilerParams(
             collective_id=0, has_side_effects=True, vmem_limit_bytes=62 * 1024 * 1024

time: 54.7 us -> 51.1 us (0.934)
  Pallas kernels: 53.5 us -> 49.8 us
    pallas_call x1, Pallas kernels: 53.5 us -> 49.8 us  [shards(): pl.pallas_call(kernel, out_shape=jax.ShapeDtypeStruct((1, rows), F32), in...]
where the time goes in v4:
time: 51.1 us; the launch traced here: 51 us
  Pallas kernels  49.8 us (97%)
  local copies, waits for them, and re-layouts  1.1 us (2%)
    pallas_call x1, Pallas kernels, shards(): pl.pallas_call(kernel, out_shape=jax.ShapeDtypeStruct((1, rows), F32), in...  49.8 us
    unnamed x3, local copies, waits for them, and re-layouts  1.1 us

profile of v4, /device:TPU:1, one launch (start us, length us, event | category | flops | bytes accessed | tf_op | source)
XLA Modules:
  0.0 51.0 jit_solution(17393909858281168396)
XLA Ops:
  0.0 49.8 %shard_map.37 = f32[1,128]{1,0:T(1,128)} custom-call(bf16[128,1536]{1,0:T(8,128)(2,1)} %emb_in.1, s32[1,128]{1,0:T(1,128)} %bitcast.2, s32[8,8]{1,0:T(8,128)} %sel_in.1), custom_call_target="tpu_custom_call" | custom-call | tf_op jit(solution)/shard_map/pallas_call | solution.py:329
  49.8 0.0 copy-start
  49.9 0.6 %copy-done = f32[1,128]{1,0:T(1,128)S(1)} copy-done((f32[1,128]{1,0:T(1,128)S(1)}, f32[1,128]{1,0:T(1,128)}, u32[]{:S(2)}) %copy-start) | copy-done | bytes 536
  50.4 0.5 %copy.5 = f32[128]{0:T(128)} copy(f32[128]{0:T(128)S(1)} %bitcast.3) | data formatting | bytes 1024
Async XLA Ops:
  49.8 0.6 %copy-start = (f32[1,128]{1,0:T(1,128)S(1)}, f32[1,128]{1,0:T(1,128)}, u32[]{:S(2)}) copy-start(f32[1,128]{1,0:T(1,128)} %shard_map.37) | copy-start | bytes 1540

commit v5 on v4

--- a/solution.py
+++ b/solution.py
@@ -40,7 +40,7 @@
 def kernel(
     emb_in, mem_in, sel_in, out,
     emb, mem, sel, sort, pick, rawx, rawy, raws, s1r, s1s, s2x, s2s, s2r, s3r, s3s, s4r, s5s, s5r, chosen,
-    points, cands, cov, acc, gs, gz,
+    points, cands, cov, gs, gz,
     loaded, zsend, xsend, ysend, ksend, psend, wrecv, crecv, gsend, grecv,
 ):
     x, y, z, k = coords()
@@ -94,21 +94,30 @@
         g = lax.rem(z + 8 - ((i % 4) * 2 + i // 4), 8)
         ids = jnp.sum(jnp.where(eye, sel[pl.ds(g, 1), :].astype(F32), 0.0), axis=1, keepdims=True)
         pickers.append(jnp.where(local == ids.astype(I32), 1.0, 0.0))
-    onehot = jnp.concatenate([sorter] + pickers, axis=0).astype(BF16)
-    low = jnp.dot(onehot, emb[:, :half], preferred_element_type=F32)
-    high = jnp.dot(onehot, emb[:, half:], preferred_element_type=F32)
-    for g in range(WIN):
-        lo, hi = slots + g * PICKS, slots + (g + 1) * PICKS
-        pick[g // 4, g % 4] = jnp.concatenate([low[lo:hi], high[lo:hi]], axis=0).astype(BF16)
-    for n in range(WIN):
-        lo, hi = n * CAP, (n + 1) * CAP
-        part = jnp.concatenate([low[lo:hi], high[lo:hi]], axis=0).astype(BF16)
-        if n == 0:
-            rawx[0, 0] = part
-        else:
-            sort[n - 1] = part
-    acc[...] = jnp.zeros_like(acc)
-
+
+    def moved(parts):
+        onehot = jnp.concatenate(parts, axis=0).astype(BF16)
+        low = jnp.dot(onehot, emb[:, :half], preferred_element_type=F32)
+        return low, jnp.dot(onehot, emb[:, half:], preferred_element_type=F32)
+
+    def sort_waves(*waves):
+        low, high = moved([sorter[n * CAP : (n + 1) * CAP] for n in waves])
+        for i, n in enumerate(waves):
+            lo, hi = i * CAP, (i + 1) * CAP
+            part = jnp.concatenate([low[lo:hi], high[lo:hi]], axis=0).astype(BF16)
+            if n == 0:
+                rawx[0, 0] = part
+            else:
+                sort[n - 1] = part
+
+    def sort_picks():
+        low, high = moved(pickers)
+        for g in range(WIN):
+            lo, hi = g * PICKS, (g + 1) * PICKS
+            pick[g // 4, g % 4] = jnp.concatenate([low[lo:hi], high[lo:hi]], axis=0).astype(BF16)
+        start(copy(pick.at[1 - k], s1r, psend.at[0], crecv.at[0], at(dk=1)))
+
+    sort_waves(1, 2)
     pl.semaphore_wait(barrier, len(peers))
 
     def start(cp):
@@ -117,8 +126,6 @@
 
     def sent(ref, sem):
         pltpu.make_async_copy(ref, ref, sem).wait()
-
-    start(copy(pick.at[1 - k], s1r, psend.at[0], crecv.at[0], at(dk=1)))
 
     def zcopy(n):
         return start(
@@ -232,26 +239,25 @@
         near = rows_dot(points[group * prow : (group + 1) * prow, :], chosen[...]) * scale
         cov[group * prow : (group + 1) * prow, :] = jnp.maximum(jnp.max(near, axis=1, keepdims=True), 0.0)
 
-    def block(lo, count, left, right):
-        cand = cands[left:right, :]
-        terms = jnp.maximum(rows_dot(points[pl.ds(lo, count), :], cand) * scale - cov[pl.ds(lo, count), :], 0.0)
-        summed = jnp.sum(terms.reshape(count // 8, 8, right - left), axis=0)
-        for b in range(left // crow, right // crow):
-            acc[b] += summed[:, b * crow - left : (b + 1) * crow - left]
-
-    def fold(p0, p1, c0, c1):
-        block(p0 * prow, (p1 - p0) * prow, c0 * crow, c1 * crow)
+    def fold():
+        terms = jnp.maximum(rows_dot(points[...], cands[...]) * scale - cov[...], 0.0)
+        return jnp.sum(terms.reshape(-1, 8, cands.shape[0]), axis=0)
 
     zs = {}
     zs[1] = zcopy(1)
     zs[2] = zcopy(2)
+    sort_waves(0)
     level0(0)
-    chosen0()
+    sort_waves(3, 4)
     zs[3] = zcopy(3)
     zs[4] = zcopy(4)
-    level0(1)
+    sort_picks()
+    sort_waves(5, 6)
     zs[5] = zcopy(5)
     zs[6] = zcopy(6)
+    sort_waves(7)
+    chosen0()
+    level0(1)
     level1(0)
     level0(2)
     chosen1()
@@ -278,20 +284,16 @@
     chosen5()
     cover(0)
     cover(1)
-    fold(0, 2, 0, 2)
     level3(3)
     assemble(2)
     cover(2)
-    fold(2, 3, 0, 3)
-    fold(0, 2, 2, 3)
     level3(4)
     assemble(3)
-    fold(0, 3, 3, 4)
     cover(3)
-    fold(3, 4, 0, 4)
+    gains = jnp.sum(fold(), axis=0, keepdims=True)
 
     for b in range(WIN // 2):
-        part = jnp.sum(acc[b], axis=0, keepdims=True)
+        part = gains[:, b * crow : (b + 1) * crow]
         gs[b] = jnp.concatenate([part, jnp.zeros((1, 256 - crow), F32)], axis=1)
     steps = (0, 1, 3, 2)
     for n in reversed(range(WIN)):
@@ -354,7 +356,6 @@
             pltpu.VMEM((8 * 8 * CAP, width), BF16),
             pltpu.VMEM((8 * 4 * CAP, width), BF16),
             pltpu.VMEM((8 * 8 * CAP, 1), F32),
-            pltpu.VMEM((4, 8, 8 * CAP), F32),
             pltpu.VMEM((4, 1, 256), F32),
             pltpu.VMEM((32, 1, 256), F32),
             dma((3,)), dma, dma, dma, dma, dma((6,)), dma((8, 8)), dma((6,)), dma, dma,

time: 51.1 us -> 50 us (0.978)
  Pallas kernels: 49.8 us -> 48.8 us
    pallas_call x1, Pallas kernels: 49.8 us -> 48.8 us  [shards(): pl.pallas_call(kernel, out_shape=jax.ShapeDtypeStruct((1, rows), F32), in...]
where the time goes in v5:
time: 50 us; the launch traced here: 49.9 us
  Pallas kernels  48.8 us (98%)
  local copies, waits for them, and re-layouts  1.1 us (2%)
    pallas_call x1, Pallas kernels, shards(): pl.pallas_call(kernel, out_shape=jax.ShapeDtypeStruct((1, rows), F32), in...  48.8 us
    unnamed x3, local copies, waits for them, and re-layouts  1.1 us

profile of v5, /device:TPU:1, one launch (start us, length us, event | category | flops | bytes accessed | tf_op | source)
XLA Modules:
  0.0 49.9 jit_solution(16646145009773031278)
XLA Ops:
  0.0 48.8 %shard_map.37 = f32[1,128]{1,0:T(1,128)} custom-call(bf16[128,1536]{1,0:T(8,128)(2,1)} %emb_in.1, s32[1,128]{1,0:T(1,128)} %bitcast.2, s32[8,8]{1,0:T(8,128)} %sel_in.1), custom_call_target="tpu_custom_call" | custom-call | tf_op jit(solution)/shard_map/pallas_call | solution.py:331
  48.8 0.0 copy-start
  48.8 0.6 %copy-done = f32[1,128]{1,0:T(1,128)S(1)} copy-done((f32[1,128]{1,0:T(1,128)S(1)}, f32[1,128]{1,0:T(1,128)}, u32[]{:S(2)}) %copy-start) | copy-done | bytes 536
  49.4 0.5 %copy.5 = f32[128]{0:T(128)} copy(f32[128]{0:T(128)S(1)} %bitcast.3) | data formatting | bytes 1024
Async XLA Ops:
  48.8 0.6 %copy-start = (f32[1,128]{1,0:T(1,128)S(1)}, f32[1,128]{1,0:T(1,128)}, u32[]{:S(2)}) copy-start(f32[1,128]{1,0:T(1,128)} %shard_map.37) | copy-start | bytes 1540
